TPU v7x, 32 devices: a whole 2x2x4 slice. The times are simulated.
32 devices in a mesh: grp: 2 (over y), tile: 8 (over z, x), tm: 2 (over core).
Axes of the slice: x: 2, y: 2, z: 4, core: 2. Of those that a mesh axis runs over, the one named last changes fastest.
Arguments:
- video: bfloat16 [8, 16, 256, 128], P(('grp', 'tm'), 'tile'), parts along dimension 0, may hold values from -60 to 60
- conv_first: bfloat16 [3, 3, 3, 128, 128], replicated, may hold values from -0.109375 to 0.109375
- conv_second: bfloat16 [3, 3, 3, 128, 128], replicated, may hold values from -0.109375 to 0.109375
- gain_first: float32 [128], replicated, may hold values from 0.1 to 1.9
- shift_first: float32 [128], replicated, may hold values from -3 to 3
- gain_second: float32 [128], replicated, may hold values from 0.1 to 1.9
- shift_second: float32 [128], replicated, may hold values from -3 to 3
- bias_second: float32 [128], replicated, may hold values from -3 to 3
Outputs:
- encoded: bfloat16 [8, 16, 256, 128], P(('grp', 'tm'), 'tile'), parts along dimension 0
There are 2 independent parts, one for each index of `grp`. A program takes and returns all parts, laid end to end along the dimension named above; an argument that names none is the same for every part. Nothing has to cross between parts.
All inputs are finite; a program needn't handle non-finite values.
Results may differ from a plain program's by a relative error of at most 0.002.
Values may be sent and summed in bfloat16 or wider, within the bound.
A program may use at most 64 MiB of HBM per device.

v0:
```python
import jax
import jax.numpy as jnp
from jax import lax
from jax.sharding import PartitionSpec as P

G = 32
EPSILON = 1e-06


def passed_along(x, axis, by):
    devices = lax.axis_size(axis)
    pairs = [(i, i + by) for i in range(devices) if 0 <= i + by < devices]
    return lax.ppermute(x, axis, pairs)


def extended_2(cells, sides, width):
    for axis, dim in sides:
        count = lax.axis_size(axis)
        ends = count - 1
        head = lax.slice_in_dim(cells, 0, width, axis=dim)
        tail = lax.slice_in_dim(cells, cells.shape[dim] - width, cells.shape[dim], axis=dim)
        cells = jnp.concatenate(
            [
                lax.ppermute(tail, axis, [(i, (i + 1) % count) for i in range(ends)]),
                cells,
                lax.ppermute(head, axis, [((i + 1) % count, i) for i in range(ends)]),
            ],
            axis=dim,
        )
    return cells


def norm_stats(values, cells_group):
    channels = values.shape[-1]
    flat = values.reshape(-1, channels)
    sums = jnp.sum(flat, axis=0).reshape(G, channels // G).sum(axis=1)
    squares = jnp.sum(flat * flat, axis=0).reshape(G, channels // G).sum(axis=1)
    totals, square_sums = lax.psum((sums, squares), ("tile", "tm"))
    center_mean = totals / cells_group
    spread = square_sums / cells_group - center_mean * center_mean
    return (center_mean, spread)


def normalize(values, center_mean, spread, gain, offset):
    channels = values.shape[-1]
    scale_group = lax.rsqrt(spread + EPSILON)
    mean_chan = jnp.repeat(center_mean, channels // G)
    scale_chan = jnp.repeat(scale_group, channels // G)
    normed = (values - mean_chan) * scale_chan * gain + offset
    return jax.nn.silu(normed).astype(jnp.bfloat16)


def causal_extend(block, received):
    front_frame = block[:1]
    repeated = jnp.concatenate([front_frame, front_frame], axis=0)
    history = jnp.where(lax.axis_index("tm") == 0, repeated, received)
    return jnp.concatenate([history, block], axis=0)


def conv_block(extended, weight):
    frame_count = extended.shape[0] - 2
    row_count = extended.shape[1] - 2
    col_count = extended.shape[2]
    channels = extended.shape[3]
    padded = jnp.pad(extended, ((0, 0), (0, 0), (1, 1), (0, 0)))
    accumulated = jnp.zeros((frame_count, row_count, col_count, weight.shape[-1]), jnp.float32)
    for time_tap in range(3):
        for row_tap in range(3):
            window = padded[time_tap : time_tap + frame_count, row_tap : row_tap + row_count]
            stacked = jnp.concatenate(
                [window[:, :, col_tap : col_tap + col_count] for col_tap in range(3)], axis=-1
            )
            kernel = weight[time_tap, row_tap].reshape(3 * channels, weight.shape[-1])
            accumulated = accumulated + jnp.dot(stacked, kernel, preferred_element_type=jnp.float32)
    return accumulated


def per_device(
    video, conv_first, conv_second, gain_first, shift_first, gain_second, shift_second, bias_second
):
    span_len, row_count, col_count, channels = video.shape
    cells_group = float(
        span_len
        * lax.axis_size("tm")
        * row_count
        * lax.axis_size("tile")
        * col_count
        * (channels // G)
    )
    source = video.astype(jnp.float32)
    mean_first, spread_first = norm_stats(source, cells_group)
    hidden_first = normalize(source, mean_first, spread_first, gain_first, shift_first)
    extended = causal_extend(hidden_first, passed_along(hidden_first, "tm", 1))
    first_out = conv_block(extended_2(extended, (("tile", 1),), 1), conv_first)
    mean_second, spread_second = norm_stats(first_out, cells_group)
    hidden_second = normalize(first_out, mean_second, spread_second, gain_second, shift_second)
    second_ext = causal_extend(hidden_second, passed_along(hidden_second, "tm", 1))
    branch = conv_block(extended_2(second_ext, (("tile", 1),), 1), conv_second)
    return (source + branch + bias_second).astype(jnp.bfloat16)


def solution(mesh):
    in_specs = (P(("grp", "tm"), "tile", None, None), P(), P(), P(), P(), P(), P(), P())
    out_specs = P(("grp", "tm"), "tile", None, None)
    return jax.shard_map(
        per_device, mesh=mesh, in_specs=in_specs, out_specs=out_specs, check_vma=False
    )
```

profile of v0, /device:TPU:0, one launch (start us, length us, event | category | flops | bytes accessed | tf_op | source)
XLA Modules:
  0.0 112.3 jit_solution(9301883458631496210)
XLA Ops:
  0.0 1.1 convert_reduce_fusion
  1.1 0.1 reshape.23
  1.2 0.1 reshape.24
  1.3 0.1 reduce_sum.73
  1.4 0.1 reduce_sum.75
  1.5 34.9 %all-reduce.3 = (f32[32]{0:T(128)S(1)}, f32[32]{0:T(128)S(1)}) all-reduce(f32[32]{0:T(128)S(1)} %reduce_sum.75, f32[32]{0:T(128)S(1)} %reduce_sum.73), channel_id=1, replica_groups=mesh['grp'=2,'tile'=8,'tm'=2] {'tile','tm'}, use_global_device_ids=true, to_apply=%region_5.0 | all-reduce | flops 64 | bytes 512 | tf_op jit(solution)/shard_map/psum | solution.py:38
  36.5 0.1 broadcast_in_dim.18
  36.5 0.1 mul.59
  36.6 0.1 broadcast_in_dim.8
  36.7 0.1 sub.26
  36.8 1.2 %fusion.116 = bf16[2,2,256,128]{3,2,1,0:T(8,128)(2,1)S(1)} fusion(bf16[2,2,256,128]{3,2,1,0:T(8,128)(2,1)} %param.8, f32[128]{0:T(128)} %param.12, f32[128]{0:T(128)} %param.11, f32[128]{0:T(128)S(1)} %mul.59, f32[128]{0:T(128)S(1)} %sub.26), kind=kLoop, calls=%fused_computation.151 | loop fusion | flops 1310720 | bytes 526336 | tf_op jit(solution)/shard_map/convert_element_type | solution.py:50
  38.0 1.4 %collective-permute-start = (bf16[2,2,256,128]{3,2,1,0:T(8,128)(2,1)S(1)}, bf16[2,2,256,128]{3,2,1,0:T(8,128)(2,1)S(1)}, u32[]{:S(2)}, u32[]{:S(2)}) collective-permute-start(bf16[2,2,256,128]{3,2,1,0:T(8,128)(2,1)S(1)} %fusion.116), channel_id=1, source_target_pairs={{0,1},{2,3},{4,5},{6,7},{8,9},{10,11},{12,13},{14,15},{16,17},{18,... | collective-permute-start | bytes 786440 | tf_op jit(solution)/shard_map/ppermute | solution.py:13
  39.5 1.1 collective-permute-done
  40.7 1.3 %collective-permute-start.1 = (bf16[4,1,256,128]{3,2,1,0:T(8,128)(2,1)S(1)}, bf16[4,1,256,128]{3,2,1,0:T(8,128)(2,1)S(1)}, u32[]{:S(2)}, u32[]{:S(2)}) collective-permute-start(bf16[4,1,256,128]{3,2,1,0:T(8,128)(2,1)S(1)} %get-tuple-element.85), channel_id=1, source_target_pairs={{0,2},{2,4},{4,6},{6,8},{8,10},{10,12},{12,14},{1,3},{3,5},{5,7},{... | collective-permute-start | bytes 786440 | tf_op jit(solution)/shard_map/ppermute | solution.py:24
  42.0 1.3 %collective-permute-start.2 = (bf16[4,1,256,128]{3,2,1,0:T(8,128)(2,1)S(1)}, bf16[4,1,256,128]{3,2,1,0:T(8,128)(2,1)S(1)}, u32[]{:S(2)}, u32[]{:S(2)}) collective-permute-start(bf16[4,1,256,128]{3,2,1,0:T(8,128)(2,1)S(1)} %get-tuple-element.86), channel_id=1, source_target_pairs={{2,0},{4,2},{6,4},{8,6},{10,8},{12,10},{14,12},{3,1},{5,3},{7,5},{... | collective-permute-start | bytes 786440 | tf_op jit(solution)/shard_map/ppermute | solution.py:26
  43.3 0.1 fusion.144
  43.4 10.6 %collective-permute-done.1 = bf16[4,1,256,128]{3,2,1,0:T(8,128)(2,1)S(1)} collective-permute-done((bf16[4,1,256,128]{3,2,1,0:T(8,128)(2,1)S(1)}, bf16[4,1,256,128]{3,2,1,0:T(8,128)(2,1)S(1)}, u32[]{:S(2)}, u32[]{:S(2)}) %collective-permute-start.1) | collective-permute-done | bytes 262176 | tf_op jit(solution)/shard_map/ppermute | solution.py:24
  54.0 0.3 fusion.11
  54.3 1.0 fusion.142
  55.2 0.1 pad_maximum_fusion.2
  55.4 0.3 fusion.147
  55.7 0.4 fusion.22
  56.0 0.4 convolution_add_fusion.15
  56.4 0.4 convolution_add_fusion.14
  56.8 0.4 convolution_add_fusion.13
  57.1 0.4 convolution_add_fusion.12
  57.5 0.4 convolution_add_fusion.11
  57.9 0.4 convolution_add_fusion.10
  58.3 0.4 convolution_add_fusion.9
  58.7 0.4 fusion.140
  59.1 0.1 reshape.25
  59.2 0.1 reduce_sum.77
  59.3 0.1 reshape.26
  59.4 0.1 reduce_sum.79
  59.5 29.5 %all-reduce.2 = (f32[32]{0:T(128)S(1)}, f32[32]{0:T(128)S(1)}) all-reduce(f32[32]{0:T(128)S(1)} %reduce_sum.79, f32[32]{0:T(128)S(1)} %reduce_sum.77), channel_id=1, replica_groups=mesh['grp'=2,'tile'=8,'tm'=2] {'tile','tm'}, use_global_device_ids=true, to_apply=%region_11.12 | all-reduce | flops 64 | bytes 512 | tf_op jit(solution)/shard_map/psum | solution.py:38
  89.0 0.1 broadcast_in_dim.20
  89.1 0.1 mul.67
  89.2 0.1 broadcast_in_dim.19
  89.3 0.1 sub.30
  89.4 0.2 multiply_convert_fusion
  89.6 0.0 copy-start.2
  89.6 1.9 %collective-permute-start.3 = (bf16[2,2,256,128]{3,2,1,0:T(8,128)(2,1)S(1)}, bf16[2,2,256,128]{3,2,1,0:T(8,128)(2,1)S(1)}, u32[]{:S(2)}, u32[]{:S(2)}) collective-permute-start(bf16[2,2,256,128]{3,2,1,0:T(8,128)(2,1)S(1)} %multiply_convert_fusion), channel_id=1, source_target_pairs={{0,1},{2,3},{4,5},{6,7},{8,9},{10,11},{12,13},{14,15},{16,17},{18,... | collective-permute-start | bytes 786440 | tf_op jit(solution)/shard_map/ppermute | solution.py:13
  91.6 1.1 collective-permute-done.3
  92.8 1.3 %collective-permute-start.4 = (bf16[4,1,256,128]{3,2,1,0:T(8,128)(2,1)S(1)}, bf16[4,1,256,128]{3,2,1,0:T(8,128)(2,1)S(1)}, u32[]{:S(2)}, u32[]{:S(2)}) collective-permute-start(bf16[4,1,256,128]{3,2,1,0:T(8,128)(2,1)S(1)} %get-tuple-element.81), channel_id=1, source_target_pairs={{0,2},{2,4},{4,6},{6,8},{8,10},{10,12},{12,14},{1,3},{3,5},{5,7},{... | collective-permute-start | bytes 786440 | tf_op jit(solution)/shard_map/ppermute | solution.py:24
  94.1 1.3 %collective-permute-start.5 = (bf16[4,1,256,128]{3,2,1,0:T(8,128)(2,1)S(1)}, bf16[4,1,256,128]{3,2,1,0:T(8,128)(2,1)S(1)}, u32[]{:S(2)}, u32[]{:S(2)}) collective-permute-start(bf16[4,1,256,128]{3,2,1,0:T(8,128)(2,1)S(1)} %get-tuple-element.82), channel_id=1, source_target_pairs={{2,0},{4,2},{6,4},{8,6},{10,8},{12,10},{14,12},{3,1},{5,3},{7,5},{... | collective-permute-start | bytes 786440 | tf_op jit(solution)/shard_map/ppermute | solution.py:26
  95.4 0.1 fusion.143
  95.5 10.6 %collective-permute-done.4 = bf16[4,1,256,128]{3,2,1,0:T(8,128)(2,1)S(1)} collective-permute-done((bf16[4,1,256,128]{3,2,1,0:T(8,128)(2,1)S(1)}, bf16[4,1,256,128]{3,2,1,0:T(8,128)(2,1)S(1)}, u32[]{:S(2)}, u32[]{:S(2)}) %collective-permute-start.4) | collective-permute-done | bytes 262176 | tf_op jit(solution)/shard_map/ppermute | solution.py:24
  106.1 0.1 pad_maximum_fusion.3
  106.2 0.1 fusion.146
  106.3 0.3 select_maximum_fusion
  106.6 1.0 fusion.141
  107.6 0.1 fusion.145
  107.7 0.4 fusion.65
  108.1 0.4 convolution_add_fusion.7
  108.4 0.4 convolution_add_fusion.6
  108.8 0.4 convolution_add_fusion.5
  109.2 0.4 convolution_add_fusion.4
  109.6 0.4 convolution_add_fusion.3
  109.9 0.4 convolution_add_fusion.2
  110.3 0.0 copy-start
  110.3 0.0 copy-start.5
  110.3 0.4 convolution_add_fusion.1
  110.7 0.6 copy-done
  111.3 1.1 fusion.3
  (18 shorter events, 0.2 us)
Async XLA Ops:
  38.0 5.3 %copy-start.1 = (bf16[3,3,3,128,128]{4,3,2,1,0:T(8,128)(2,1)S(1)}, bf16[3,3,3,128,128]{4,3,2,1,0:T(8,128)(2,1)}, u32[]{:S(2)}) copy-start(bf16[3,3,3,128,128]{4,3,2,1,0:T(8,128)(2,1)} %param.9) | copy-start | bytes 2654212
  38.0 2.6 %collective-permute-start = (bf16[2,2,256,128]{3,2,1,0:T(8,128)(2,1)S(1)}, bf16[2,2,256,128]{3,2,1,0:T(8,128)(2,1)S(1)}, u32[]{:S(2)}, u32[]{:S(2)}) collective-permute-start(bf16[2,2,256,128]{3,2,1,0:T(8,128)(2,1)S(1)} %fusion.116), channel_id=1, source_target_pairs={{0,1},{2,3},{4,5},{6,7},{8,9},{10,11},{12,13},{14,15},{16,17},{18,... | collective-permute-start | bytes 786440 | tf_op jit(solution)/shard_map/ppermute | solution.py:13
  40.7 13.3 %collective-permute-start.1 = (bf16[4,1,256,128]{3,2,1,0:T(8,128)(2,1)S(1)}, bf16[4,1,256,128]{3,2,1,0:T(8,128)(2,1)S(1)}, u32[]{:S(2)}, u32[]{:S(2)}) collective-permute-start(bf16[4,1,256,128]{3,2,1,0:T(8,128)(2,1)S(1)} %get-tuple-element.85), channel_id=1, source_target_pairs={{0,2},{2,4},{4,6},{6,8},{8,10},{10,12},{12,14},{1,3},{3,5},{5,7},{... | collective-permute-start | bytes 786440 | tf_op jit(solution)/shard_map/ppermute | solution.py:24
  42.0 12.0 %collective-permute-start.2 = (bf16[4,1,256,128]{3,2,1,0:T(8,128)(2,1)S(1)}, bf16[4,1,256,128]{3,2,1,0:T(8,128)(2,1)S(1)}, u32[]{:S(2)}, u32[]{:S(2)}) collective-permute-start(bf16[4,1,256,128]{3,2,1,0:T(8,128)(2,1)S(1)} %get-tuple-element.86), channel_id=1, source_target_pairs={{2,0},{4,2},{6,4},{8,6},{10,8},{12,10},{14,12},{3,1},{5,3},{7,5},{... | collective-permute-start | bytes 786440 | tf_op jit(solution)/shard_map/ppermute | solution.py:26
  58.6 30.8 %copy-start.3 = (f32[128]{0:T(128)S(1)}, f32[128]{0:T(128)}, u32[]{:S(2)}) copy-start(f32[128]{0:T(128)} %param.14) | copy-start | bytes 1540
  58.7 30.8 %copy-start.4 = (f32[128]{0:T(128)S(1)}, f32[128]{0:T(128)}, u32[]{:S(2)}) copy-start(f32[128]{0:T(128)} %param.13) | copy-start | bytes 1540
  89.6 5.8 %copy-start.2 = (bf16[3,3,3,128,128]{4,3,2,1,0:T(8,128)(2,1)S(1)}, bf16[3,3,3,128,128]{4,3,2,1,0:T(8,128)(2,1)}, u32[]{:S(2)}) copy-start(bf16[3,3,3,128,128]{4,3,2,1,0:T(8,128)(2,1)} %param.10) | copy-start | bytes 2654212
  89.6 3.1 %collective-permute-start.3 = (bf16[2,2,256,128]{3,2,1,0:T(8,128)(2,1)S(1)}, bf16[2,2,256,128]{3,2,1,0:T(8,128)(2,1)S(1)}, u32[]{:S(2)}, u32[]{:S(2)}) collective-permute-start(bf16[2,2,256,128]{3,2,1,0:T(8,128)(2,1)S(1)} %multiply_convert_fusion), channel_id=1, source_target_pairs={{0,1},{2,3},{4,5},{6,7},{8,9},{10,11},{12,13},{14,15},{16,17},{18,... | collective-permute-start | bytes 786440 | tf_op jit(solution)/shard_map/ppermute | solution.py:13
  92.8 13.3 %collective-permute-start.4 = (bf16[4,1,256,128]{3,2,1,0:T(8,128)(2,1)S(1)}, bf16[4,1,256,128]{3,2,1,0:T(8,128)(2,1)S(1)}, u32[]{:S(2)}, u32[]{:S(2)}) collective-permute-start(bf16[4,1,256,128]{3,2,1,0:T(8,128)(2,1)S(1)} %get-tuple-element.81), channel_id=1, source_target_pairs={{0,2},{2,4},{4,6},{6,8},{8,10},{10,12},{12,14},{1,3},{3,5},{5,7},{... | collective-permute-start | bytes 786440 | tf_op jit(solution)/shard_map/ppermute | solution.py:24
  94.1 12.0 %collective-permute-start.5 = (bf16[4,1,256,128]{3,2,1,0:T(8,128)(2,1)S(1)}, bf16[4,1,256,128]{3,2,1,0:T(8,128)(2,1)S(1)}, u32[]{:S(2)}, u32[]{:S(2)}) collective-permute-start(bf16[4,1,256,128]{3,2,1,0:T(8,128)(2,1)S(1)} %get-tuple-element.82), channel_id=1, source_target_pairs={{2,0},{4,2},{6,4},{8,6},{10,8},{12,10},{14,12},{3,1},{5,3},{7,5},{... | collective-permute-start | bytes 786440 | tf_op jit(solution)/shard_map/ppermute | solution.py:26
  110.3 1.0 copy-start
  110.3 0.9 copy-start.5
where the time goes:
time: 113 us; the launch traced here: 112 us
  blocking collectives  64.4 us (57%)
  waiting for transfers between devices  23.4 us (21%)
  starting transfers between devices  8.55 us (8%)
  matrix products  7.35 us (7%)
  local copies, waits for them, and re-layouts  4.33 us (4%)
  other arithmetic  3.9 us (3%)
    psum x2, blocking collectives, norm_stats(): totals, square_sums = lax.psum((sums, squares), ('tile', 'tm'))  64.4 us
    ppermute x2, waiting for transfers between devices, extended_2(): lax.ppermute(tail, axis, [(i, (i + 1) % count) for i in range(ends)])  21.2 us
    dot_general x18, matrix products, conv_block(): jnp.dot(stacked, kernel, preferred_element_type=jnp.float32)  7.35 us
    ppermute x2, starting transfers between devices, passed_along(): return lax.ppermute(x, axis, pairs)  3.35 us
    ppermute x2, starting transfers between devices, extended_2(): lax.ppermute(tail, axis, [(i, (i + 1) % count) for i in range(ends)])  2.61 us
    ppermute x2, starting transfers between devices, extended_2(): lax.ppermute(head, axis, [((i + 1) % count, i) for i in range(ends)])  2.58 us
    slice x5, local copies, waits for them, and re-layouts, conv_block(): window[:, :, col_tap:col_tap + col_count]  2.46 us
  transfers between devices with their start and end apart: 6, of which 4 were waited for; matrix products, arithmetic and copies ran while one was open for 0% of the time, Pallas kernels for 0%

commit v1 on v0

--- a/solution.py
+++ b/solution.py
@@ -35,7 +35,13 @@
     flat = values.reshape(-1, channels)
     sums = jnp.sum(flat, axis=0).reshape(G, channels // G).sum(axis=1)
     squares = jnp.sum(flat * flat, axis=0).reshape(G, channels // G).sum(axis=1)
-    totals, square_sums = lax.psum((sums, squares), ("tile", "tm"))
+
+    def zone_launch(x_in, bus_axis, mesh_name):
+        for hop_no in (bus_axis, mesh_name):
+            x_in = lax.psum(x_in, axis_name=hop_no)
+        return x_in
+
+    totals, square_sums = zone_launch((sums, squares), "tm", "tile")
     center_mean = totals / cells_group
     spread = square_sums / cells_group - center_mean * center_mean
     return (center_mean, spread)

time: 113 us -> 95.5 us (0.85)
  blocking collectives: 64.4 us -> 47.6 us
    psum x2 -> x4, blocking collectives: 64.4 us -> 47.6 us  [zone_launch(): x_in = lax.psum(x_in, axis_name=hop_no)]
where the time goes in v1:
time: 95.5 us; the launch traced here: 95.1 us
  blocking collectives  47.6 us (50%)
  waiting for transfers between devices  23.2 us (24%)
  starting transfers between devices  8.23 us (9%)
  matrix products  7.36 us (8%)
  local copies, waits for them, and re-layouts  4.33 us (5%)
  other arithmetic  3.9 us (4%)
    psum x4, blocking collectives, zone_launch(): x_in = lax.psum(x_in, axis_name=hop_no)  47.6 us
    ppermute x2, waiting for transfers between devices, extended_2(): lax.ppermute(tail, axis, [(i, (i + 1) % count) for i in range(ends)])  21 us
    dot_general x18, matrix products, conv_block(): jnp.dot(stacked, kernel, preferred_element_type=jnp.float32)  7.36 us
    ppermute x2, starting transfers between devices, passed_along(): return lax.ppermute(x, axis, pairs)  2.87 us
    ppermute x2, starting transfers between devices, extended_2(): lax.ppermute(tail, axis, [(i, (i + 1) % count) for i in range(ends)])  2.77 us
    ppermute x2, starting transfers between devices, extended_2(): lax.ppermute(head, axis, [((i + 1) % count, i) for i in range(ends)])  2.58 us
    slice x5, local copies, waits for them, and re-layouts, conv_block(): window[:, :, col_tap:col_tap + col_count]  2.46 us
    ppermute x2, waiting for transfers between devices, passed_along(): return lax.ppermute(x, axis, pairs)  2.21 us
  transfers between devices with their start and end apart: 6, of which 4 were waited for; matrix products, arithmetic and copies ran while one was open for 0% of the time, Pallas kernels for 0%

profile of v1, /device:TPU:0, one launch (start us, length us, event | category | flops | bytes accessed | tf_op | source)
XLA Modules:
  0.0 95.1 jit_solution(59439621330333198)
XLA Ops:
  0.0 1.1 %convert_reduce_fusion = (f32[128]{0:T(128)S(1)}, f32[128]{0:T(128)S(1)}) fusion(bf16[2,2,256,128]{3,2,1,0:T(8,128)(2,1)} %param.8), kind=kLoop, calls=%fused_computation.36 | loop fusion | flops 524032 | bytes 263168 | tf_op jit(solution)/shard_map/reduce_sum | solution.py:36
  1.1 0.1 reshape.23
  1.2 0.1 reshape.24
  1.3 0.1 reduce_sum.73
  1.4 0.1 reduce_sum.75
  1.5 2.6 %all-reduce.5 = (f32[32]{0:T(128)S(1)}, f32[32]{0:T(128)S(1)}) all-reduce(f32[32]{0:T(128)S(1)} %reduce_sum.75, f32[32]{0:T(128)S(1)} %reduce_sum.73), channel_id=1, replica_groups=mesh['grp'=2,'tile'=8,'tm'=2] {'tm'}, use_global_device_ids=true, to_apply=%region_6.0 | all-reduce | flops 64 | bytes 512 | tf_op jit(solution)/shard_map/psum | solution.py:41
  4.1 23.0 %all-reduce.3 = (f32[32]{0:T(128)S(1)}, f32[32]{0:T(128)S(1)}) all-reduce(f32[32]{0:T(128)S(1)} %get-tuple-element.15, f32[32]{0:T(128)S(1)} %get-tuple-element.16), channel_id=1, replica_groups=mesh['grp'=2,'tile'=8,'tm'=2] {'tile'}, use_global_device_ids=true, to_apply=%region_7.0 | all-reduce | flops 64 | bytes 512 | tf_op jit(solution)/shard_map/psum | solution.py:41
  27.1 0.1 broadcast_in_dim.18
  27.2 0.1 mul.59
  27.3 0.1 broadcast_in_dim.8
  27.4 0.1 sub.26
  27.5 1.2 %fusion.116 = bf16[2,2,256,128]{3,2,1,0:T(8,128)(2,1)S(1)} fusion(bf16[2,2,256,128]{3,2,1,0:T(8,128)(2,1)} %param.8, f32[128]{0:T(128)} %param.12, f32[128]{0:T(128)} %param.11, f32[128]{0:T(128)S(1)} %mul.59, f32[128]{0:T(128)S(1)} %sub.26), kind=kLoop, calls=%fused_computation.151 | loop fusion | flops 1310720 | bytes 526336 | tf_op jit(solution)/shard_map/convert_element_type | solution.py:56
  28.7 1.4 %collective-permute-start = (bf16[2,2,256,128]{3,2,1,0:T(8,128)(2,1)S(1)}, bf16[2,2,256,128]{3,2,1,0:T(8,128)(2,1)S(1)}, u32[]{:S(2)}, u32[]{:S(2)}) collective-permute-start(bf16[2,2,256,128]{3,2,1,0:T(8,128)(2,1)S(1)} %fusion.116), channel_id=1, source_target_pairs={{0,1},{2,3},{4,5},{6,7},{8,9},{10,11},{12,13},{14,15},{16,17},{18,... | collective-permute-start | bytes 786440 | tf_op jit(solution)/shard_map/ppermute | solution.py:13
  30.1 1.1 %collective-permute-done = bf16[2,2,256,128]{3,2,1,0:T(8,128)(2,1)S(1)} collective-permute-done((bf16[2,2,256,128]{3,2,1,0:T(8,128)(2,1)S(1)}, bf16[2,2,256,128]{3,2,1,0:T(8,128)(2,1)S(1)}, u32[]{:S(2)}, u32[]{:S(2)}) %collective-permute-start) | collective-permute-done | bytes 262176 | tf_op jit(solution)/shard_map/ppermute | solution.py:13
  31.3 1.3 %collective-permute-start.1 = (bf16[4,1,256,128]{3,2,1,0:T(8,128)(2,1)S(1)}, bf16[4,1,256,128]{3,2,1,0:T(8,128)(2,1)S(1)}, u32[]{:S(2)}, u32[]{:S(2)}) collective-permute-start(bf16[4,1,256,128]{3,2,1,0:T(8,128)(2,1)S(1)} %get-tuple-element.89), channel_id=1, source_target_pairs={{0,2},{2,4},{4,6},{6,8},{8,10},{10,12},{12,14},{1,3},{3,5},{5,7},{... | collective-permute-start | bytes 786440 | tf_op jit(solution)/shard_map/ppermute | solution.py:24
  32.6 1.3 %collective-permute-start.2 = (bf16[4,1,256,128]{3,2,1,0:T(8,128)(2,1)S(1)}, bf16[4,1,256,128]{3,2,1,0:T(8,128)(2,1)S(1)}, u32[]{:S(2)}, u32[]{:S(2)}) collective-permute-start(bf16[4,1,256,128]{3,2,1,0:T(8,128)(2,1)S(1)} %get-tuple-element.90), channel_id=1, source_target_pairs={{2,0},{4,2},{6,4},{8,6},{10,8},{12,10},{14,12},{3,1},{5,3},{7,5},{... | collective-permute-start | bytes 786440 | tf_op jit(solution)/shard_map/ppermute | solution.py:26
  33.9 0.1 fusion.144
  34.0 10.6 %collective-permute-done.1 = bf16[4,1,256,128]{3,2,1,0:T(8,128)(2,1)S(1)} collective-permute-done((bf16[4,1,256,128]{3,2,1,0:T(8,128)(2,1)S(1)}, bf16[4,1,256,128]{3,2,1,0:T(8,128)(2,1)S(1)}, u32[]{:S(2)}, u32[]{:S(2)}) %collective-permute-start.1) | collective-permute-done | bytes 262176 | tf_op jit(solution)/shard_map/ppermute | solution.py:24
  44.6 0.3 fusion.11
  44.9 1.0 %fusion.142 = (bf16[2,2,256,128]{3,2,1,0:T(8,128)(2,1)S(1)}, bf16[2,2,256,128]{3,2,1,0:T(8,128)(2,1)S(1)}, bf16[2,2,256,128]{3,2,1,0:T(8,128)(2,1)S(1)}, bf16[2,...) fusion(bf16[4,4,258,128]{3,2,1,0:T(8,128)(2,1)S(1)} %fusion.11), kind=kLoop, calls=%fused_computation.185 | loop fusion | bytes 9437184 | tf_op jit(solution)/shard_map/slice | solution.py:77
  45.9 0.1 pad_maximum_fusion.2
  46.0 0.3 fusion.147
  46.3 0.4 fusion.22
  46.7 0.4 convolution_add_fusion.15
  47.1 0.4 convolution_add_fusion.14
  47.4 0.4 convolution_add_fusion.13
  47.8 0.4 convolution_add_fusion.12
  48.2 0.4 convolution_add_fusion.11
  48.6 0.4 convolution_add_fusion.10
  48.9 0.4 convolution_add_fusion.9
  49.3 0.0 copy-start.3
  49.3 0.4 fusion.140
  49.7 0.1 reshape.25
  49.8 0.1 reduce_sum.77
  50.0 0.1 reshape.26
  50.1 0.1 reduce_sum.79
  50.2 2.5 %all-reduce.4 = (f32[32]{0:T(128)S(1)}, f32[32]{0:T(128)S(1)}) all-reduce(f32[32]{0:T(128)S(1)} %reduce_sum.79, f32[32]{0:T(128)S(1)} %reduce_sum.77), channel_id=1, replica_groups=mesh['grp'=2,'tile'=8,'tm'=2] {'tm'}, use_global_device_ids=true, to_apply=%region_14.15 | all-reduce | flops 64 | bytes 512 | tf_op jit(solution)/shard_map/psum | solution.py:41
  52.7 19.6 %all-reduce.2 = (f32[32]{0:T(128)S(1)}, f32[32]{0:T(128)S(1)}) all-reduce(f32[32]{0:T(128)S(1)} %get-tuple-element.13, f32[32]{0:T(128)S(1)} %get-tuple-element.14), channel_id=1, replica_groups=mesh['grp'=2,'tile'=8,'tm'=2] {'tile'}, use_global_device_ids=true, to_apply=%region_15.16 | all-reduce | flops 64 | bytes 512 | tf_op jit(solution)/shard_map/psum | solution.py:41
  72.3 0.1 broadcast_in_dim.20
  72.3 0.1 mul.67
  72.4 0.1 broadcast_in_dim.19
  72.5 0.1 sub.30
  72.7 0.2 multiply_convert_fusion
  72.9 1.4 %collective-permute-start.3 = (bf16[2,2,256,128]{3,2,1,0:T(8,128)(2,1)S(1)}, bf16[2,2,256,128]{3,2,1,0:T(8,128)(2,1)S(1)}, u32[]{:S(2)}, u32[]{:S(2)}) collective-permute-start(bf16[2,2,256,128]{3,2,1,0:T(8,128)(2,1)S(1)} %multiply_convert_fusion), channel_id=1, source_target_pairs={{0,1},{2,3},{4,5},{6,7},{8,9},{10,11},{12,13},{14,15},{16,17},{18,... | collective-permute-start | bytes 786440 | tf_op jit(solution)/shard_map/ppermute | solution.py:13
  74.3 1.1 %collective-permute-done.3 = bf16[2,2,256,128]{3,2,1,0:T(8,128)(2,1)S(1)} collective-permute-done((bf16[2,2,256,128]{3,2,1,0:T(8,128)(2,1)S(1)}, bf16[2,2,256,128]{3,2,1,0:T(8,128)(2,1)S(1)}, u32[]{:S(2)}, u32[]{:S(2)}) %collective-permute-start.3) | collective-permute-done | bytes 262176 | tf_op jit(solution)/shard_map/ppermute | solution.py:13
  75.5 1.5 %collective-permute-start.4 = (bf16[4,1,256,128]{3,2,1,0:T(8,128)(2,1)S(1)}, bf16[4,1,256,128]{3,2,1,0:T(8,128)(2,1)S(1)}, u32[]{:S(2)}, u32[]{:S(2)}) collective-permute-start(bf16[4,1,256,128]{3,2,1,0:T(8,128)(2,1)S(1)} %get-tuple-element.85), channel_id=1, source_target_pairs={{0,2},{2,4},{4,6},{6,8},{8,10},{10,12},{12,14},{1,3},{3,5},{5,7},{... | collective-permute-start | bytes 786440 | tf_op jit(solution)/shard_map/ppermute | solution.py:24
  77.0 1.3 %collective-permute-start.5 = (bf16[4,1,256,128]{3,2,1,0:T(8,128)(2,1)S(1)}, bf16[4,1,256,128]{3,2,1,0:T(8,128)(2,1)S(1)}, u32[]{:S(2)}, u32[]{:S(2)}) collective-permute-start(bf16[4,1,256,128]{3,2,1,0:T(8,128)(2,1)S(1)} %get-tuple-element.86), channel_id=1, source_target_pairs={{2,0},{4,2},{6,4},{8,6},{10,8},{12,10},{14,12},{3,1},{5,3},{7,5},{... | collective-permute-start | bytes 786440 | tf_op jit(solution)/shard_map/ppermute | solution.py:26
  78.3 0.1 fusion.143
  78.4 10.4 %collective-permute-done.4 = bf16[4,1,256,128]{3,2,1,0:T(8,128)(2,1)S(1)} collective-permute-done((bf16[4,1,256,128]{3,2,1,0:T(8,128)(2,1)S(1)}, bf16[4,1,256,128]{3,2,1,0:T(8,128)(2,1)S(1)}, u32[]{:S(2)}, u32[]{:S(2)}) %collective-permute-start.4) | collective-permute-done | bytes 262176 | tf_op jit(solution)/shard_map/ppermute | solution.py:24
  88.8 0.1 pad_maximum_fusion.3
  88.9 0.1 fusion.146
  89.0 0.3 select_maximum_fusion
  89.3 1.0 %fusion.141 = (bf16[2,2,256,128]{3,2,1,0:T(8,128)(2,1)S(1)}, bf16[2,2,256,128]{3,2,1,0:T(8,128)(2,1)S(1)}, bf16[2,2,256,128]{3,2,1,0:T(8,128)(2,1)S(1)}, bf16[2,...) fusion(bf16[4,4,258,128]{3,2,1,0:T(8,128)(2,1)S(1)} %select_max, ...), kind=kLoop, calls=%fused_computation.184 | loop fusion | bytes 9437184 | tf_op jit(solution)/shard_map/slice | solution.py:77
  90.3 0.1 fusion.145
  90.4 0.4 fusion.65
  90.8 0.4 convolution_add_fusion.7
  91.2 0.4 convolution_add_fusion.6
  91.6 0.4 convolution_add_fusion.5
  91.9 0.4 convolution_add_fusion.4
  92.3 0.4 convolution_add_fusion.3
  92.7 0.4 convolution_add_fusion.2
  93.1 0.4 convolution_add_fusion.1
  93.5 0.6 copy-done
  94.0 1.1 %fusion.3 = bf16[2,2,256,128]{3,2,1,0:T(8,128)(2,1)} fusion(f32[2,2,256,128]{3,2,1,0:T(8,128)S(1)} %convolution_add_fusion.1, bf16[384,128,1,1]{1,0,3,2:T(8,128)(2,1)S(1)} %bitcast.109, bf16[2,2,256,128]{3,2,1,0:T(8,128)(2,1)S(1)} %copy-done, bf16[2,2,256,128]{3,2,1,0:T(8,128)(2,1)S(1)} %get-tuple-element.34, ...), kind=kOutput, calls=%fused_computation.21 | convolution fusion | flops 103677952 | bytes 1933824 | tf_op jit(solution)/shard_map/dot_general | solution.py:80
  (20 shorter events, 0.2 us)
Async XLA Ops:
  28.6 5.3 %copy-start.1 = (bf16[3,3,3,128,128]{4,3,2,1,0:T(8,128)(2,1)S(1)}, bf16[3,3,3,128,128]{4,3,2,1,0:T(8,128)(2,1)}, u32[]{:S(2)}) copy-start(bf16[3,3,3,128,128]{4,3,2,1,0:T(8,128)(2,1)} %param.9) | copy-start | bytes 2654212
  28.7 2.6 %collective-permute-start = (bf16[2,2,256,128]{3,2,1,0:T(8,128)(2,1)S(1)}, bf16[2,2,256,128]{3,2,1,0:T(8,128)(2,1)S(1)}, u32[]{:S(2)}, u32[]{:S(2)}) collective-permute-start(bf16[2,2,256,128]{3,2,1,0:T(8,128)(2,1)S(1)} %fusion.116), channel_id=1, source_target_pairs={{0,1},{2,3},{4,5},{6,7},{8,9},{10,11},{12,13},{14,15},{16,17},{18,... | collective-permute-start | bytes 786440 | tf_op jit(solution)/shard_map/ppermute | solution.py:13
  31.3 13.3 %collective-permute-start.1 = (bf16[4,1,256,128]{3,2,1,0:T(8,128)(2,1)S(1)}, bf16[4,1,256,128]{3,2,1,0:T(8,128)(2,1)S(1)}, u32[]{:S(2)}, u32[]{:S(2)}) collective-permute-start(bf16[4,1,256,128]{3,2,1,0:T(8,128)(2,1)S(1)} %get-tuple-element.89), channel_id=1, source_target_pairs={{0,2},{2,4},{4,6},{6,8},{8,10},{10,12},{12,14},{1,3},{3,5},{5,7},{... | collective-permute-start | bytes 786440 | tf_op jit(solution)/shard_map/ppermute | solution.py:24
  32.6 12.0 %collective-permute-start.2 = (bf16[4,1,256,128]{3,2,1,0:T(8,128)(2,1)S(1)}, bf16[4,1,256,128]{3,2,1,0:T(8,128)(2,1)S(1)}, u32[]{:S(2)}, u32[]{:S(2)}) collective-permute-start(bf16[4,1,256,128]{3,2,1,0:T(8,128)(2,1)S(1)} %get-tuple-element.90), channel_id=1, source_target_pairs={{2,0},{4,2},{6,4},{8,6},{10,8},{12,10},{14,12},{3,1},{5,3},{7,5},{... | collective-permute-start | bytes 786440 | tf_op jit(solution)/shard_map/ppermute | solution.py:26
  49.3 23.3 %copy-start.3 = (f32[128]{0:T(128)S(1)}, f32[128]{0:T(128)}, u32[]{:S(2)}) copy-start(f32[128]{0:T(128)} %param.14) | copy-start | bytes 1540
  49.3 23.3 %copy-start.4 = (f32[128]{0:T(128)S(1)}, f32[128]{0:T(128)}, u32[]{:S(2)}) copy-start(f32[128]{0:T(128)} %param.13) | copy-start | bytes 1540
  72.8 5.5 %copy-start.2 = (bf16[3,3,3,128,128]{4,3,2,1,0:T(8,128)(2,1)S(1)}, bf16[3,3,3,128,128]{4,3,2,1,0:T(8,128)(2,1)}, u32[]{:S(2)}) copy-start(bf16[3,3,3,128,128]{4,3,2,1,0:T(8,128)(2,1)} %param.10) | copy-start | bytes 2654212
  72.9 2.6 %collective-permute-start.3 = (bf16[2,2,256,128]{3,2,1,0:T(8,128)(2,1)S(1)}, bf16[2,2,256,128]{3,2,1,0:T(8,128)(2,1)S(1)}, u32[]{:S(2)}, u32[]{:S(2)}) collective-permute-start(bf16[2,2,256,128]{3,2,1,0:T(8,128)(2,1)S(1)} %multiply_convert_fusion), channel_id=1, source_target_pairs={{0,1},{2,3},{4,5},{6,7},{8,9},{10,11},{12,13},{14,15},{16,17},{18,... | collective-permute-start | bytes 786440 | tf_op jit(solution)/shard_map/ppermute | solution.py:13
  75.5 13.3 %collective-permute-start.4 = (bf16[4,1,256,128]{3,2,1,0:T(8,128)(2,1)S(1)}, bf16[4,1,256,128]{3,2,1,0:T(8,128)(2,1)S(1)}, u32[]{:S(2)}, u32[]{:S(2)}) collective-permute-start(bf16[4,1,256,128]{3,2,1,0:T(8,128)(2,1)S(1)} %get-tuple-element.85), channel_id=1, source_target_pairs={{0,2},{2,4},{4,6},{6,8},{8,10},{10,12},{12,14},{1,3},{3,5},{5,7},{... | collective-permute-start | bytes 786440 | tf_op jit(solution)/shard_map/ppermute | solution.py:24
  77.0 11.8 %collective-permute-start.5 = (bf16[4,1,256,128]{3,2,1,0:T(8,128)(2,1)S(1)}, bf16[4,1,256,128]{3,2,1,0:T(8,128)(2,1)S(1)}, u32[]{:S(2)}, u32[]{:S(2)}) collective-permute-start(bf16[4,1,256,128]{3,2,1,0:T(8,128)(2,1)S(1)} %get-tuple-element.86), channel_id=1, source_target_pairs={{2,0},{4,2},{6,4},{8,6},{10,8},{12,10},{14,12},{3,1},{5,3},{7,5},{... | collective-permute-start | bytes 786440 | tf_op jit(solution)/shard_map/ppermute | solution.py:26
  93.1 1.0 %copy-start = (bf16[2,2,256,128]{3,2,1,0:T(8,128)(2,1)S(1)}, bf16[2,2,256,128]{3,2,1,0:T(8,128)(2,1)}, u32[]{:S(2)}) copy-start(bf16[2,2,256,128]{3,2,1,0:T(8,128)(2,1)} %param.8) | copy-start | bytes 786436
  93.1 0.9 copy-start.5
